TPU v7x, 32 devices: a whole 2x2x4 slice. The times are simulated.
32 devices in a mesh: groups: 2 (over y), cols: 4 (over z), rows: 2 (over x), pair: 2 (over core).
Axes of the slice: x: 2, y: 2, z: 4, core: 2. Of those that a mesh axis runs over, the one named last changes fastest.
Arguments:
- clip_inputs: bfloat16 [2, 512, 1024], P(None, 'groups', 'rows'), parts along dimension 1, may hold values from -6 to 6
- head_weights: bfloat16 [2, 1024, 1024], P(None, 'rows', 'cols'), may hold values from -0.1875 to 0.1875
- owner_slot: int32 [512], P('groups'), parts along dimension 0, may hold values from 0 to 255, each once
- sign_seed: int32 [1], replicated, may hold values from 0 to 1073741823
Outputs:
- features: float32 [512, 1024], P(('groups', 'cols', 'rows'), 'pair'), parts along dimension 0
There are 2 independent parts, one for each index of `groups`. A program takes and returns all parts, laid end to end along the dimension named above; an argument that names none is the same for every part. Nothing has to cross between parts.
Inputs may be any that keep to these rules, and one draw needn't show every extreme that they name: `owner_slot`: each of 0 to 255 appears exactly once.
All inputs are finite; a program needn't handle non-finite values.
Results may differ from a plain program's by a relative error of at most 0.0029.
Values sent between devices are 32-bit elements; how exact they have to be, the bound alone decides.
A program may use at most 64 MiB of HBM per device.

v0:
```python
import jax
import jax.numpy as jnp
from jax import lax
from jax.sharding import PartitionSpec as P

D = 1024
PROJ = 1024


logit_scale = 14.0


def sign_values(seed_value, k_index, a_index, b_index, full_width):
    m_index = jnp.arange(2, dtype=jnp.int32).reshape(2, 1, 1, 1)
    k_grid = k_index.reshape(1, 1, -1, 1)
    a_grid = a_index.reshape(1, -1, 1, 1)
    b_grid = b_index.reshape(1, 1, 1, -1)
    width = jnp.int32(full_width)
    mixer = jnp.int32(73244475)
    golden = jnp.int32(-1640531535)
    numbers = ((k_grid * 2 + m_index) * width + a_grid) * width + b_grid
    hashed = numbers + seed_value * golden
    hashed = hashed * mixer
    hashed = hashed ^ lax.shift_right_logical(hashed, jnp.int32(16))
    hashed = hashed * mixer
    hashed = hashed ^ lax.shift_right_logical(hashed, jnp.int32(16))
    low_bit = lax.shift_right_logical(hashed, jnp.int32(8)) & jnp.int32(1)
    return (1.0 - 2.0 * low_bit.astype(jnp.float32)) * full_width ** (-0.5)


def head_grads(embedded):
    inv_norm = 1.0 / jnp.sqrt(jnp.sum(embedded * embedded, axis=2, keepdims=True) + 1e-06)
    unit = embedded * inv_norm
    scores = logit_scale * jnp.dot(
        unit[0], unit[1].T, precision=lax.Precision.HIGHEST, preferred_element_type=jnp.float32
    )
    expo = jnp.exp(scores - logit_scale)
    row_soft = expo / jnp.sum(expo, axis=1, keepdims=True)
    col_soft = (expo / jnp.sum(expo, axis=0, keepdims=True)).T
    own_row = jnp.diagonal(row_soft)[:, None]
    own_col = jnp.diagonal(col_soft)[:, None]
    half_scale = 0.5 * logit_scale
    grad_audio = half_scale * (
        jnp.dot(
            row_soft, unit[1], precision=lax.Precision.HIGHEST, preferred_element_type=jnp.float32
        )
        - (2.0 - own_col) * unit[1]
    )
    grad_video = half_scale * (
        jnp.dot(
            col_soft, unit[0], precision=lax.Precision.HIGHEST, preferred_element_type=jnp.float32
        )
        - (2.0 - own_row) * unit[0]
    )
    unit_grad = jnp.stack([grad_audio, grad_video])
    along = jnp.sum(unit * unit_grad, axis=2, keepdims=True)
    return ((unit_grad - unit * along) * inv_norm).astype(jnp.bfloat16)


def per_device(clip_inputs, head_weights, owner_slot, sign_seed):
    clip_count = clip_inputs.shape[1]
    input_part = clip_inputs.shape[2]
    proj_part = PROJ // lax.axis_size("pair")
    input_start = lax.axis_index("rows") * input_part
    proj_start = lax.axis_index("pair") * proj_part
    partial_value = jnp.einsum(
        "mia,mab->mib", clip_inputs, head_weights, preferred_element_type=jnp.float32
    )
    summed = lax.psum(partial_value, "rows")
    embedded = lax.all_gather(summed, "cols", axis=2, tiled=True)
    grads_all = head_grads(embedded)
    clip_order = jnp.argsort(owner_slot)
    seed_value = sign_seed[0]
    a_index = input_start + jnp.arange(input_part, dtype=jnp.int32)
    col_count = lax.axis_size("cols")
    row_count_axis = lax.axis_size("rows")
    k_part = proj_part // col_count
    k_start = proj_start + lax.axis_index("cols") * k_part
    per_dev = clip_count // (col_count * row_count_axis)
    arranged = jnp.transpose(
        clip_order.reshape(col_count, row_count_axis, per_dev), (1, 0, 2)
    ).reshape(clip_count)
    chosen_inputs = jnp.take(clip_inputs, arranged, axis=1)
    chosen_grads = jnp.take(grads_all, arranged, axis=1).astype(jnp.float32)
    b_full = jnp.arange(D, dtype=jnp.int32)
    small_block = 4

    def full_block(block_index):
        k_index = k_start + block_index * small_block + jnp.arange(small_block, dtype=jnp.int32)
        sign_block = sign_values(seed_value, k_index, a_index, b_full, D).astype(jnp.bfloat16)
        product = jnp.einsum(
            "mna,makb->mnkb", chosen_inputs, sign_block, preferred_element_type=jnp.float32
        )
        return jnp.einsum("mnkb,mnb->nk", product, chosen_grads)

    blocks = lax.map(full_block, jnp.arange(k_part // small_block, dtype=jnp.int32))
    local_terms = jnp.transpose(blocks, (1, 0, 2)).reshape(clip_count, k_part)
    reduced = lax.psum_scatter(local_terms, "rows", scatter_dimension=0, tiled=True)
    return lax.all_to_all(reduced, "cols", split_axis=0, concat_axis=1, tiled=True)


def solution(mesh):
    placed = (P(None, "groups", "rows"), P(None, "rows", "cols"), P("groups"), P())
    return jax.shard_map(
        per_device,
        mesh=mesh,
        in_specs=placed,
        out_specs=P(("groups", "cols", "rows"), "pair"),
        check_vma=False,
    )
```

profile of v0, /device:TPU:0, one launch (start us, length us, event | category | flops | bytes accessed | tf_op | source)
XLA Modules:
  0.0 590.1 jit_solution(10560732391093313533)
XLA Ops:
  9.8 31.4 %all-reduce.2.cloned.1.call-done = f32[2,256,256]{2,1,0:T(8,128)} async-done(((f32[2,256,256]{2,1,0:T(8,128)}), f32[2,256,256]{2,1,0:T(8,128)}) %all-reduce.2.cloned.1.call-update) | async-done | bytes 524304 | tf_op jit(solution)/shard_map/psum | solution.py:69
  48.7 40.1 %all-gather.2.cloned.1.call-done = f32[2,256,1024]{2,1,0:T(8,128)} async-done(((f32[2,256,256]{2,1,0:T(8,128)}), f32[2,256,1024]{2,1,0:T(8,128)}) %all-gather.2.cloned.1.call-update) | async-done | bytes 2097168 | tf_op jit(solution)/shard_map/all_gather | solution.py:70
  113.3 448.7 %while.13 = (s32[]{:T(128)}, f32[32,256,4]{1,2,0:T(4,128)S(1)}, s32[32]{0:T(128)S(1)}, s32[]{:T(128)}, s32[]{:T(128)}, /*index=5*/bf16[2,256,512]{2,1,0:T(8,128)...) while((s32[]{:T(128)}, f32[32,256,4]{1,2,0:T(4,128)S(1)}, ...), condition=%wide.region_7.8_spmd.clone, body=%wide.region_6.7_spmd.clone.sunk | while | flops 2214600192 | bytes 6865145 | solution.py:96
  116.5 10.8 %fusion.59 = f32[256,4]{0,1:T(4,128)S(1)} fusion(f32[256,1024,2]{0,1,2:T(8,128)} %copy.27, s32[]{:T(128)} %get-tuple-element.243, s32[2,512,4]{1,2,0:T(4,128)S(1)} %add_multiply_fusion.8, bf16[2,256,512]{2,1,0:T(8,128)(2,1)S(1)} %get-tuple-element.244), kind=kOutput, calls=%fused_computation.21.clone.1 | convolution fusion | flops 2214591488 | bytes 2641924 | tf_op jit(solution)/shard_map/while/body/eval_jaxpr/mna,makb->mnkb/dot_general | solution.py:91
  130.5 10.8 %fusion.59 = f32[256,4]{0,1:T(4,128)S(1)} fusion(f32[256,1024,2]{0,1,2:T(8,128)} %copy.27, s32[]{:T(128)} %get-tuple-element.243, s32[2,512,4]{1,2,0:T(4,128)S(1)} %add_multiply_fusion.8, bf16[2,256,512]{2,1,0:T(8,128)(2,1)S(1)} %get-tuple-element.244), kind=kOutput, calls=%fused_computation.21.clone.1 | convolution fusion | flops 2214591488 | bytes 2641924 | tf_op jit(solution)/shard_map/while/body/eval_jaxpr/mna,makb->mnkb/dot_general | solution.py:91
  158.6 10.8 %fusion.59 = f32[256,4]{0,1:T(4,128)S(1)} fusion(f32[256,1024,2]{0,1,2:T(8,128)} %copy.27, s32[]{:T(128)} %get-tuple-element.243, s32[2,512,4]{1,2,0:T(4,128)S(1)} %add_multiply_fusion.8, bf16[2,256,512]{2,1,0:T(8,128)(2,1)S(1)} %get-tuple-element.244), kind=kOutput, calls=%fused_computation.21.clone.1 | convolution fusion | flops 2214591488 | bytes 2641924 | tf_op jit(solution)/shard_map/while/body/eval_jaxpr/mna,makb->mnkb/dot_general | solution.py:91
  172.6 10.8 %fusion.59 = f32[256,4]{0,1:T(4,128)S(1)} fusion(f32[256,1024,2]{0,1,2:T(8,128)} %copy.27, s32[]{:T(128)} %get-tuple-element.243, s32[2,512,4]{1,2,0:T(4,128)S(1)} %add_multiply_fusion.8, bf16[2,256,512]{2,1,0:T(8,128)(2,1)S(1)} %get-tuple-element.244), kind=kOutput, calls=%fused_computation.21.clone.1 | convolution fusion | flops 2214591488 | bytes 2641924 | tf_op jit(solution)/shard_map/while/body/eval_jaxpr/mna,makb->mnkb/dot_general | solution.py:91
  186.6 10.8 %fusion.59 = f32[256,4]{0,1:T(4,128)S(1)} fusion(f32[256,1024,2]{0,1,2:T(8,128)} %copy.27, s32[]{:T(128)} %get-tuple-element.243, s32[2,512,4]{1,2,0:T(4,128)S(1)} %add_multiply_fusion.8, bf16[2,256,512]{2,1,0:T(8,128)(2,1)S(1)} %get-tuple-element.244), kind=kOutput, calls=%fused_computation.21.clone.1 | convolution fusion | flops 2214591488 | bytes 2641924 | tf_op jit(solution)/shard_map/while/body/eval_jaxpr/mna,makb->mnkb/dot_general | solution.py:91
  200.6 10.8 %fusion.59 = f32[256,4]{0,1:T(4,128)S(1)} fusion(f32[256,1024,2]{0,1,2:T(8,128)} %copy.27, s32[]{:T(128)} %get-tuple-element.243, s32[2,512,4]{1,2,0:T(4,128)S(1)} %add_multiply_fusion.8, bf16[2,256,512]{2,1,0:T(8,128)(2,1)S(1)} %get-tuple-element.244), kind=kOutput, calls=%fused_computation.21.clone.1 | convolution fusion | flops 2214591488 | bytes 2641924 | tf_op jit(solution)/shard_map/while/body/eval_jaxpr/mna,makb->mnkb/dot_general | solution.py:91
  214.6 10.8 %fusion.59 = f32[256,4]{0,1:T(4,128)S(1)} fusion(f32[256,1024,2]{0,1,2:T(8,128)} %copy.27, s32[]{:T(128)} %get-tuple-element.243, s32[2,512,4]{1,2,0:T(4,128)S(1)} %add_multiply_fusion.8, bf16[2,256,512]{2,1,0:T(8,128)(2,1)S(1)} %get-tuple-element.244), kind=kOutput, calls=%fused_computation.21.clone.1 | convolution fusion | flops 2214591488 | bytes 2641924 | tf_op jit(solution)/shard_map/while/body/eval_jaxpr/mna,makb->mnkb/dot_general | solution.py:91
  228.7 10.8 %fusion.59 = f32[256,4]{0,1:T(4,128)S(1)} fusion(f32[256,1024,2]{0,1,2:T(8,128)} %copy.27, s32[]{:T(128)} %get-tuple-element.243, s32[2,512,4]{1,2,0:T(4,128)S(1)} %add_multiply_fusion.8, bf16[2,256,512]{2,1,0:T(8,128)(2,1)S(1)} %get-tuple-element.244), kind=kOutput, calls=%fused_computation.21.clone.1 | convolution fusion | flops 2214591488 | bytes 2641924 | tf_op jit(solution)/shard_map/while/body/eval_jaxpr/mna,makb->mnkb/dot_general | solution.py:91
  242.7 10.8 %fusion.59 = f32[256,4]{0,1:T(4,128)S(1)} fusion(f32[256,1024,2]{0,1,2:T(8,128)} %copy.27, s32[]{:T(128)} %get-tuple-element.243, s32[2,512,4]{1,2,0:T(4,128)S(1)} %add_multiply_fusion.8, bf16[2,256,512]{2,1,0:T(8,128)(2,1)S(1)} %get-tuple-element.244), kind=kOutput, calls=%fused_computation.21.clone.1 | convolution fusion | flops 2214591488 | bytes 2641924 | tf_op jit(solution)/shard_map/while/body/eval_jaxpr/mna,makb->mnkb/dot_general | solution.py:91
  270.7 10.8 %fusion.59 = f32[256,4]{0,1:T(4,128)S(1)} fusion(f32[256,1024,2]{0,1,2:T(8,128)} %copy.27, s32[]{:T(128)} %get-tuple-element.243, s32[2,512,4]{1,2,0:T(4,128)S(1)} %add_multiply_fusion.8, bf16[2,256,512]{2,1,0:T(8,128)(2,1)S(1)} %get-tuple-element.244), kind=kOutput, calls=%fused_computation.21.clone.1 | convolution fusion | flops 2214591488 | bytes 2641924 | tf_op jit(solution)/shard_map/while/body/eval_jaxpr/mna,makb->mnkb/dot_general | solution.py:91
  284.8 10.8 %fusion.59 = f32[256,4]{0,1:T(4,128)S(1)} fusion(f32[256,1024,2]{0,1,2:T(8,128)} %copy.27, s32[]{:T(128)} %get-tuple-element.243, s32[2,512,4]{1,2,0:T(4,128)S(1)} %add_multiply_fusion.8, bf16[2,256,512]{2,1,0:T(8,128)(2,1)S(1)} %get-tuple-element.244), kind=kOutput, calls=%fused_computation.21.clone.1 | convolution fusion | flops 2214591488 | bytes 2641924 | tf_op jit(solution)/shard_map/while/body/eval_jaxpr/mna,makb->mnkb/dot_general | solution.py:91
  298.8 10.8 %fusion.59 = f32[256,4]{0,1:T(4,128)S(1)} fusion(f32[256,1024,2]{0,1,2:T(8,128)} %copy.27, s32[]{:T(128)} %get-tuple-element.243, s32[2,512,4]{1,2,0:T(4,128)S(1)} %add_multiply_fusion.8, bf16[2,256,512]{2,1,0:T(8,128)(2,1)S(1)} %get-tuple-element.244), kind=kOutput, calls=%fused_computation.21.clone.1 | convolution fusion | flops 2214591488 | bytes 2641924 | tf_op jit(solution)/shard_map/while/body/eval_jaxpr/mna,makb->mnkb/dot_general | solution.py:91
  326.8 10.8 %fusion.59 = f32[256,4]{0,1:T(4,128)S(1)} fusion(f32[256,1024,2]{0,1,2:T(8,128)} %copy.27, s32[]{:T(128)} %get-tuple-element.243, s32[2,512,4]{1,2,0:T(4,128)S(1)} %add_multiply_fusion.8, bf16[2,256,512]{2,1,0:T(8,128)(2,1)S(1)} %get-tuple-element.244), kind=kOutput, calls=%fused_computation.21.clone.1 | convolution fusion | flops 2214591488 | bytes 2641924 | tf_op jit(solution)/shard_map/while/body/eval_jaxpr/mna,makb->mnkb/dot_general | solution.py:91
  340.9 10.8 %fusion.59 = f32[256,4]{0,1:T(4,128)S(1)} fusion(f32[256,1024,2]{0,1,2:T(8,128)} %copy.27, s32[]{:T(128)} %get-tuple-element.243, s32[2,512,4]{1,2,0:T(4,128)S(1)} %add_multiply_fusion.8, bf16[2,256,512]{2,1,0:T(8,128)(2,1)S(1)} %get-tuple-element.244), kind=kOutput, calls=%fused_computation.21.clone.1 | convolution fusion | flops 2214591488 | bytes 2641924 | tf_op jit(solution)/shard_map/while/body/eval_jaxpr/mna,makb->mnkb/dot_general | solution.py:91
  382.9 10.8 %fusion.59 = f32[256,4]{0,1:T(4,128)S(1)} fusion(f32[256,1024,2]{0,1,2:T(8,128)} %copy.27, s32[]{:T(128)} %get-tuple-element.243, s32[2,512,4]{1,2,0:T(4,128)S(1)} %add_multiply_fusion.8, bf16[2,256,512]{2,1,0:T(8,128)(2,1)S(1)} %get-tuple-element.244), kind=kOutput, calls=%fused_computation.21.clone.1 | convolution fusion | flops 2214591488 | bytes 2641924 | tf_op jit(solution)/shard_map/while/body/eval_jaxpr/mna,makb->mnkb/dot_general | solution.py:91
  396.9 10.8 %fusion.59 = f32[256,4]{0,1:T(4,128)S(1)} fusion(f32[256,1024,2]{0,1,2:T(8,128)} %copy.27, s32[]{:T(128)} %get-tuple-element.243, s32[2,512,4]{1,2,0:T(4,128)S(1)} %add_multiply_fusion.8, bf16[2,256,512]{2,1,0:T(8,128)(2,1)S(1)} %get-tuple-element.244), kind=kOutput, calls=%fused_computation.21.clone.1 | convolution fusion | flops 2214591488 | bytes 2641924 | tf_op jit(solution)/shard_map/while/body/eval_jaxpr/mna,makb->mnkb/dot_general | solution.py:91
  439.0 10.8 %fusion.59 = f32[256,4]{0,1:T(4,128)S(1)} fusion(f32[256,1024,2]{0,1,2:T(8,128)} %copy.27, s32[]{:T(128)} %get-tuple-element.243, s32[2,512,4]{1,2,0:T(4,128)S(1)} %add_multiply_fusion.8, bf16[2,256,512]{2,1,0:T(8,128)(2,1)S(1)} %get-tuple-element.244), kind=kOutput, calls=%fused_computation.21.clone.1 | convolution fusion | flops 2214591488 | bytes 2641924 | tf_op jit(solution)/shard_map/while/body/eval_jaxpr/mna,makb->mnkb/dot_general | solution.py:91
  453.0 10.8 %fusion.59 = f32[256,4]{0,1:T(4,128)S(1)} fusion(f32[256,1024,2]{0,1,2:T(8,128)} %copy.27, s32[]{:T(128)} %get-tuple-element.243, s32[2,512,4]{1,2,0:T(4,128)S(1)} %add_multiply_fusion.8, bf16[2,256,512]{2,1,0:T(8,128)(2,1)S(1)} %get-tuple-element.244), kind=kOutput, calls=%fused_computation.21.clone.1 | convolution fusion | flops 2214591488 | bytes 2641924 | tf_op jit(solution)/shard_map/while/body/eval_jaxpr/mna,makb->mnkb/dot_general | solution.py:91
  495.1 10.8 %fusion.59 = f32[256,4]{0,1:T(4,128)S(1)} fusion(f32[256,1024,2]{0,1,2:T(8,128)} %copy.27, s32[]{:T(128)} %get-tuple-element.243, s32[2,512,4]{1,2,0:T(4,128)S(1)} %add_multiply_fusion.8, bf16[2,256,512]{2,1,0:T(8,128)(2,1)S(1)} %get-tuple-element.244), kind=kOutput, calls=%fused_computation.21.clone.1 | convolution fusion | flops 2214591488 | bytes 2641924 | tf_op jit(solution)/shard_map/while/body/eval_jaxpr/mna,makb->mnkb/dot_general | solution.py:91
  509.1 10.8 %fusion.59 = f32[256,4]{0,1:T(4,128)S(1)} fusion(f32[256,1024,2]{0,1,2:T(8,128)} %copy.27, s32[]{:T(128)} %get-tuple-element.243, s32[2,512,4]{1,2,0:T(4,128)S(1)} %add_multiply_fusion.8, bf16[2,256,512]{2,1,0:T(8,128)(2,1)S(1)} %get-tuple-element.244), kind=kOutput, calls=%fused_computation.21.clone.1 | convolution fusion | flops 2214591488 | bytes 2641924 | tf_op jit(solution)/shard_map/while/body/eval_jaxpr/mna,makb->mnkb/dot_general | solution.py:91
  551.2 10.8 %fusion.59 = f32[256,4]{0,1:T(4,128)S(1)} fusion(f32[256,1024,2]{0,1,2:T(8,128)} %copy.27, s32[]{:T(128)} %get-tuple-element.243, s32[2,512,4]{1,2,0:T(4,128)S(1)} %add_multiply_fusion.8, bf16[2,256,512]{2,1,0:T(8,128)(2,1)S(1)} %get-tuple-element.244), kind=kOutput, calls=%fused_computation.21.clone.1 | convolution fusion | flops 2214591488 | bytes 2641924 | tf_op jit(solution)/shard_map/while/body/eval_jaxpr/mna,makb->mnkb/dot_general | solution.py:91
  (293 shorter events, 256.2 us)
Async XLA Ops:
  6.5 1.0 copy-start
  6.5 34.7 %copy-start.7 = (s32[256]{0:T(256)S(1)}, s32[256]{0:T(256)}, u32[]{:S(2)}) copy-start(s32[256]{0:T(256)} %param.8) | copy-start | bytes 3076
  6.5 34.6 %all-reduce.2.cloned.1.call-start = ((), (), s32[]{:S(2)}) async-start(), calls=%async_computation.2 | async-start | bytes 1048576 | tf_op jit(solution)/shard_map/psum | solution.py:69
  9.7 79.1 %all-gather.2.cloned.1.call-start = ((), (), s32[]{:S(2)}) async-start(), calls=%async_computation.3 | async-start | bytes 2621440 | tf_op jit(solution)/shard_map/all_gather | solution.py:70
  41.2 530.6 %reduce-scatter.2.cloned.1.call-start = ((), (), s32[]{:S(2)}) async-start(), calls=%async_computation.4 | async-start | bytes 196608 | tf_op jit(solution)/shard_map/reduce_scatter | solution.py:98
  47.8 0.9 copy-start.5
  88.8 2.2 copy-start.1
  91.2 1.4 copy-start.2
  100.0 2.9 copy-start.3
  106.9 3.9 copy-start.6
  112.2 1.0 copy-start.4
Sparse Core Ops, SparseCore 0:
  9.9 31.2 all-reduce.1
  42.8 45.9 all-gather.1
  562.8 8.9 reduce-scatter.1
where the time goes:
time: 591 us; the launch traced here: 590 us
  matrix products  352 us (60%)
  local copies, waits for them, and re-layouts  96.9 us (16%)
  waiting for transfers between devices  80.7 us (14%)
  loops' own time  22.5 us (4%)
  other arithmetic  14.3 us (2%)
  between operations  14 us (2%)
  blocking collectives  10.1 us (2%)
    dot_general x32, matrix products, full_block(): jnp.einsum('mna,makb->mnkb', chosen_inputs, sign_block, preferred_element...  344 us
    while x32, local copies, waits for them, and re-layouts  59.9 us
    all_gather x1, waiting for transfers between devices, per_device(): embedded = lax.all_gather(summed, 'cols', axis=2, tiled=True)  40.1 us
    psum x1, waiting for transfers between devices, per_device(): summed = lax.psum(partial_value, 'rows')  31.4 us
    another operation x1, loops' own time, per_device(): lax.map(full_block, jnp.arange(k_part // small_block, dtype=jnp.int32))  22.5 us
    dynamic_slice x32, local copies, waits for them, and re-layouts, per_device(): lax.map(full_block, jnp.arange(k_part // small_block, dtype=jnp.int32))  18.8 us
  transfers between devices with their start and end apart: 3, of which 3 were waited for; matrix products, arithmetic and copies ran while one was open for 1% of the time, Pallas kernels for 0%

commit v1 on v0

v1 whole, which is shorter than its diff:
```python
import functools

import jax
import jax.numpy as jnp
from jax import lax
from jax.experimental import pallas as pl
from jax.experimental.pallas import tpu as pltpu
from jax.sharding import PartitionSpec as P

D = 1024
PROJ = 1024
MIXER = 73244475
GOLDEN = -1640531535
RESIDUES = 16
GROUP = 8

logit_scale = 14.0


def wrap32(value):
    value &= 0xFFFFFFFF
    return value - (1 << 32) if value >= (1 << 31) else value


def shift_right(value, amount):
    return lax.shift_right_logical(value, jnp.full((), amount, value.dtype))


def project_kernel(base_ref, x_ref, g_ref, o_ref, top_ref, low_ref, add_ref, gain_ref, even_ref, odd_ref):
    res = pl.program_id(0)
    m = pl.program_id(1)
    b_part, a_part = top_ref.shape
    steps = o_ref.shape[1]
    i32, i16 = jnp.int32, jnp.int16
    start = base_ref[0] + (res * 2 + m) * i32(D * D)
    rows = 32

    def prepare(step, carry):
        at = pl.ds(pl.multiple_of(step * rows, rows), rows)
        b_index = lax.broadcasted_iota(i32, (rows, a_part), 0) + step * rows
        a_index = lax.broadcasted_iota(i32, (rows, a_part), 1)
        h1 = (start + a_index * D + b_index) * i32(MIXER)
        h2 = h1 ^ shift_right(h1, 16)
        bit8 = shift_right(h2 * i32(MIXER), 8) & 1
        high = shift_right(h1, 16)
        w = high & 0x1FF
        fixed = ((w << 16) | ((h1 & 0x1FF) ^ w)) * i32(MIXER)
        top_ref[at, :] = (high & 0xFE00).astype(i16)
        low_ref[at, :] = (h1 & 0xFE00).astype(i16)
        add_ref[at, :] = (shift_right(fixed, 9) + (bit8 << 15)).astype(i16)
        return carry

    lax.fori_loop(0, b_part // rows, prepare, 0)
    gain_ref[...] = g_ref[m].astype(jnp.float32) * (D**-0.5)

    def fill(ref, step):
        for u in range(GROUP):
            shift = shift_right((step * GROUP + u) * i32(wrap32(MIXER << 25)), 16).astype(i16)
            mixed = shift_right((top_ref[...] + shift) ^ low_ref[...], 9)
            value = mixed * i16((MIXER & 0xFFFF) - 0x10000) + add_ref[...]
            ref[u * b_part : (u + 1) * b_part, :] = jnp.where(value < 0, jnp.bfloat16(-1), jnp.bfloat16(1))

    def use(ref, step):
        product = jnp.dot(ref[...], x_ref[m], preferred_element_type=jnp.float32)
        n = product.shape[1]
        terms = product.reshape(GROUP, b_part // 8, 8, n) * gain_ref[...].reshape(1, b_part // 8, 8, n)
        total = jnp.sum(jnp.sum(terms, axis=1), axis=1)
        o_ref[res, step] = jnp.where(m == 0, 0.0, o_ref[res, step]) + total

    fill(even_ref, 0)

    def body(t, carry):
        use(even_ref, 2 * t)
        fill(odd_ref, 2 * t + 1)
        use(odd_ref, 2 * t + 1)
        fill(even_ref, 2 * t + 2)
        return carry

    lax.fori_loop(0, steps // 2, body, 0)


def project(base, x, g, k_count):
    _, a_part, n = x.shape
    b_part = g.shape[1]
    steps = k_count // (RESIDUES * GROUP)
    whole = pl.BlockSpec(memory_space=pltpu.VMEM)
    return pl.pallas_call(
        project_kernel,
        grid=(RESIDUES, 2),
        in_specs=[pl.BlockSpec(memory_space=pltpu.SMEM), whole, whole],
        out_specs=whole,
        out_shape=jax.ShapeDtypeStruct((RESIDUES, steps, GROUP, n), jnp.float32),
        scratch_shapes=[pltpu.VMEM((b_part, a_part), jnp.int16)] * 3
        + [pltpu.VMEM((b_part, n), jnp.float32)]
        + [pltpu.VMEM((GROUP * b_part, a_part), jnp.bfloat16)] * 2,
        compiler_params=pltpu.CompilerParams(vmem_limit_bytes=48 * 2**20),
    )(base, x, g)


def head_grads(embedded):
    clips = embedded.shape[2]
    exact = dict(precision=lax.Precision.HIGHEST, preferred_element_type=jnp.float32)
    raw = lax.dot_general(embedded[0], embedded[1], (((0,), (0,)), ((), ())), **exact)
    squares = jnp.sum(embedded * embedded, axis=1)
    both = lax.psum(jnp.concatenate([raw, squares], axis=0), "cols")
    inv_norm = 1.0 / jnp.sqrt(both[clips:] + 1e-06)
    unit = embedded * inv_norm[:, None, :]
    cosine = both[:clips] * inv_norm[0][:, None] * inv_norm[1][None, :]
    expo = jnp.exp(logit_scale * cosine - logit_scale)
    row_soft = expo / jnp.sum(expo, axis=1, keepdims=True)
    col_soft = expo / jnp.sum(expo, axis=0, keepdims=True)
    rest_row = 2.0 - jnp.diagonal(row_soft)
    rest_col = 2.0 - jnp.diagonal(col_soft)
    own = jnp.diagonal(cosine)
    half_scale = 0.5 * logit_scale
    pull_audio = lax.dot_general(unit[1], row_soft, (((1,), (1,)), ((), ())), **exact)
    pull_video = lax.dot_general(unit[0], col_soft, (((1,), (0,)), ((), ())), **exact)
    unit_grad = half_scale * jnp.stack([pull_audio - rest_col * unit[1], pull_video - rest_row * unit[0]])
    along_audio = jnp.sum(row_soft * cosine, axis=1) - rest_col * own
    along_video = jnp.sum(col_soft * cosine, axis=0) - rest_row * own
    along = half_scale * jnp.stack([along_audio, along_video])[:, None, :]
    return ((unit_grad - unit * along) * inv_norm[:, None, :]).astype(jnp.bfloat16)


def per_device(clip_inputs, head_weights, owner_slot, sign_seed):
    clip_count = clip_inputs.shape[1]
    a_part = clip_inputs.shape[2]
    b_part = head_weights.shape[2]
    k_part = PROJ // lax.axis_size("pair")
    a_start = lax.axis_index("rows") * a_part
    b_start = lax.axis_index("cols") * b_part
    k_start = lax.axis_index("pair") * k_part
    slots = jnp.arange(clip_count, dtype=jnp.int32)
    chosen = (owner_slot[None, :] == slots[:, None]).astype(jnp.bfloat16)
    x = jnp.einsum("mia,si->mas", clip_inputs, chosen, preferred_element_type=jnp.float32).astype(jnp.bfloat16)
    partial_value = jnp.einsum("mab,mas->mbs", head_weights, x, preferred_element_type=jnp.float32)
    grads = head_grads(lax.psum(partial_value, "rows"))
    base = sign_seed * jnp.int32(GOLDEN) + (k_start * (2 * D * D) + a_start * D + b_start).astype(jnp.int32)
    phi = project(base, x, grads, k_part)
    phi = jnp.transpose(phi.reshape(RESIDUES, -1, clip_count), (2, 1, 0)).reshape(clip_count, k_part)
    return lax.psum_scatter(phi, ("cols", "rows"), scatter_dimension=0, tiled=True)


def solution(mesh):
    placed = (P(None, "groups", "rows"), P(None, "rows", "cols"), P("groups"), P())
    return jax.shard_map(
        per_device,
        mesh=mesh,
        in_specs=placed,
        out_specs=P(("groups", "cols", "rows"), "pair"),
        check_vma=False,
    )
```

time: 591 us -> 304 us (0.51)
  matrix products: 352 us -> 4.79 us
  Pallas kernels: 0 us -> 143 us
  local copies, waits for them, and re-layouts: 96.9 us -> 9.38 us
  waiting for transfers between devices: 80.7 us -> 129 us
  loops' own time: 22.5 us -> 0 us
  other arithmetic: 14.3 us -> 3.09 us
  blocking collectives: 10.1 us -> 0 us
    dot_general x36 -> x5, matrix products: 352 us -> 4.79 us  [the longest x1 1.68 us: head_grads(): lax.dot_general(embedded[0], embedded[1], (((0,), (0,)), ((), ())), **exact)]
    pallas_call x0 -> x1, Pallas kernels: none -> 143 us  [project(): pl.pallas_call(project_kernel, grid=(RESIDUES, 2), in_specs=[pl.BlockSpec...]
    while x32 -> x0, local copies, waits for them, and re-layouts: 59.9 us -> none
    reduce_scatter x1, waiting for transfers between devices: 9.13 us -> 62.5 us  [per_device(): lax.psum_scatter(phi, ('cols', 'rows'), scatter_dimension=0, tiled=True)]
    all_gather x1 -> x0, waiting for transfers between devices: 40.1 us -> none  [per_device(): embedded = lax.all_gather(summed, 'cols', axis=2, tiled=True)]
    psum x1 -> x2, waiting for transfers between devices: 31.4 us -> 66.3 us  [the longest x1 34.9 us: head_grads(): both = lax.psum(jnp.concatenate([raw, squares], axis=0), 'cols')]
    another operation x1 -> x0, loops' own time: 22.5 us -> none  [per_device(): lax.map(full_block, jnp.arange(k_part // small_block, dtype=jnp.int32))]
    dynamic_slice x32 -> x0, local copies, waits for them, and re-layouts: 18.8 us -> none  [per_device(): lax.map(full_block, jnp.arange(k_part // small_block, dtype=jnp.int32))]
  transfers between devices with their start and end apart: 3 -> 3, of which waited for: 3 -> 3; matrix products, arithmetic and copies ran while one was open for 1% -> 0% of each run, Pallas kernels for 0% -> 0%
where the time goes in v1:
time: 304 us; the launch traced here: 303 us
  Pallas kernels  143 us (47%)
  waiting for transfers between devices  129 us (42%)
  between operations  13.9 us (5%)
  local copies, waits for them, and re-layouts  9.38 us (3%)
  matrix products  4.79 us (2%)
  other arithmetic  3.09 us (1%)
    pallas_call x1, Pallas kernels, project(): pl.pallas_call(project_kernel, grid=(RESIDUES, 2), in_specs=[pl.BlockSpec...  143 us
    reduce_scatter x1, waiting for transfers between devices, per_device(): lax.psum_scatter(phi, ('cols', 'rows'), scatter_dimension=0, tiled=True)  62.5 us
    psum x1, waiting for transfers between devices, head_grads(): both = lax.psum(jnp.concatenate([raw, squares], axis=0), 'cols')  34.9 us
    psum x1, waiting for transfers between devices, per_device(): grads = head_grads(lax.psum(partial_value, 'rows'))  31.4 us
  transfers between devices with their start and end apart: 3, of which 3 were waited for; matrix products, arithmetic and copies ran while one was open for 0% of the time, Pallas kernels for 0%

profile of v1, /device:TPU:0, one launch (start us, length us, event | category | flops | bytes accessed | tf_op | source)
XLA Modules:
  0.0 303.3 jit_solution(8582095707828302372)
XLA Ops:
  6.5 1.0 copy-done
  7.6 1.0 fusion.x_ref
  8.6 1.2 convolution_bitcast_fusion
  9.8 0.0 all-reduce.5.cloned.1.call-start
  9.9 31.4 %all-reduce.3.cloned.1.call-done = f32[2,256,256]{2,1,0:T(8,128)} async-done(((f32[2,256,256]{2,1,0:T(8,128)}), f32[2,256,256]{2,1,0:T(8,128)}) %all-reduce.3.cloned.1.call-update) | async-done | bytes 524304 | tf_op jit(solution)/shard_map/psum | solution.py:137
  41.3 1.7 fusion.7
  43.0 0.1 multiply_reduce_fusion
  43.0 0.7 pad_maximum_fusion
  43.7 0.0 reduce-scatter.4.cloned.1.call-start
  44.5 34.9 %all-reduce.5.cloned.1.call-done = f32[258,256]{1,0:T(8,128)} async-done(((f32[258,256]{1,0:T(8,128)}), f32[258,256]{1,0:T(8,128)}) %all-reduce.5.cloned.1.call-update) | async-done | bytes 264208 | tf_op jit(solution)/shard_map/psum | solution.py:105
  79.4 0.7 fusion.13
  80.1 1.2 fusion.12
  81.2 0.2 multiply_reduce_fusion.2
  81.4 0.1 multiply_reduce_fusion.1
  81.5 2.3 gather_fusion.2
  83.9 2.3 gather_fusion
  86.2 2.3 gather_fusion.1
  88.6 0.5 fusion.2
  89.1 0.4 fusion.1
  89.6 0.1 fusion.5.g_ref
  89.7 143.3 %shard_map.46 = f32[16,4,8,256]{3,2,1,0:T(8,128)S(1)} custom-call(s32[1]{0:T(128)S(6)} %add.36.base_ref, bf16[2,512,256]{2,1,0:T(8,128)(2,1)S(1)} %fusion.x_ref, bf16[2,256,256]{2,1,0:T(8,128)(2,1)S(1)} %fusion.5.g_ref), custom_call_target="tpu_custom_call" | custom-call | tf_op jit(solution)/shard_map/pallas_call | solution.py:87
  233.0 0.3 copy.17
  233.3 1.0 copy.22
  234.3 62.5 %reduce-scatter.4.cloned.1.call-done = f32[32,512]{1,0:T(8,128)} async-done(((f32[256,512]{1,0:T(8,128)}), f32[32,512]{1,0:T(8,128)}) %reduce-scatter.4.cloned.1.call-update) | async-done | bytes 65552 | tf_op jit(solution)/shard_map/reduce_scatter | solution.py:141
  (14 shorter events, 0.1 us)
Async XLA Ops:
  6.5 1.0 copy-start
  6.5 2.1 copy-start.2
  6.5 34.7 %all-reduce.3.cloned.1.call-start = ((), (), s32[]{:S(2)}) async-start(), calls=%async_computation.1 | async-start | bytes 1048576 | tf_op jit(solution)/shard_map/psum | solution.py:137
  9.8 69.6 %all-reduce.5.cloned.1.call-start = ((), (), s32[]{:S(2)}) async-start(), calls=%async_computation.2 | async-start | bytes 540672 | tf_op jit(solution)/shard_map/psum | solution.py:105
  41.3 1.7 copy-start.1
  43.7 253.0 %reduce-scatter.4.cloned.1.call-start = ((), (), s32[]{:S(2)}) async-start(), calls=%async_computation.3 | async-start | bytes 589824 | tf_op jit(solution)/shard_map/reduce_scatter | solution.py:141
Sparse Core Ops, SparseCore 0:
  9.9 31.2 all-reduce.2
  43.9 35.4 all-reduce.4
  234.4 62.3 reduce-scatter.3

commit v2 on v1

--- a/solution.py
+++ b/solution.py
@@ -97,21 +97,137 @@
     )(base, x, g)
 
 
+MESH = pl.DeviceIdType.MESH
+
+
+def sum_kernel(axis, size, part_ref, o_ref, slots_ref, send_sem, recv_sem, swap_send, swap_recv):
+    me = lax.axis_index(axis)
+    half = lax.axis_index("pair")
+    peers = [lax.rem(me + offset, size) for offset in range(1, size)]
+    barrier = pltpu.get_barrier_semaphore()
+    for peer in peers:
+        pl.semaphore_signal(barrier, inc=1, device_id={axis: peer}, device_id_type=MESH)
+    pl.semaphore_signal(barrier, inc=1, device_id={"pair": 1 - half}, device_id_type=MESH)
+    pl.semaphore_wait(barrier, size)
+    copies = []
+    for at, peer in enumerate(peers):
+        copy = pltpu.make_async_remote_copy(
+            src_ref=part_ref.at[half],
+            dst_ref=slots_ref.at[at],
+            send_sem=send_sem.at[at],
+            recv_sem=recv_sem.at[at],
+            device_id={axis: peer},
+            device_id_type=MESH,
+        )
+        copy.start()
+        copies.append(copy)
+    total = part_ref[half]
+    for at, copy in enumerate(copies):
+        copy.wait()
+        total = total + slots_ref[at]
+    o_ref[half] = total
+    swap = pltpu.make_async_remote_copy(
+        src_ref=o_ref.at[half],
+        dst_ref=o_ref.at[half],
+        send_sem=swap_send,
+        recv_sem=swap_recv,
+        device_id={"pair": 1 - half},
+        device_id_type=MESH,
+    )
+    swap.start()
+    swap.wait()
+
+
+def sum_over(part, axis, collective_id):
+    size = lax.axis_size(axis)
+    _, height, n = part.shape
+    whole = pl.BlockSpec(memory_space=pltpu.VMEM)
+    return pl.pallas_call(
+        functools.partial(sum_kernel, axis, size),
+        in_specs=[whole],
+        out_specs=whole,
+        out_shape=jax.ShapeDtypeStruct(part.shape, jnp.float32),
+        scratch_shapes=[
+            pltpu.VMEM((size - 1, height, n), jnp.float32),
+            pltpu.SemaphoreType.DMA((size - 1,)),
+            pltpu.SemaphoreType.DMA((size - 1,)),
+            pltpu.SemaphoreType.DMA,
+            pltpu.SemaphoreType.DMA,
+        ],
+        compiler_params=pltpu.CompilerParams(
+            collective_id=collective_id, has_side_effects=True, vmem_limit_bytes=32 * 2**20
+        ),
+    )(part)
+
+
+def scatter_kernel(cols, rows, phi_ref, o_ref, slots_ref, send_sem, recv_sem):
+    size = cols * rows
+    me = lax.axis_index("cols") * rows + lax.axis_index("rows")
+    peers = [lax.rem(me + offset, size) for offset in range(1, size)]
+    places = [{"cols": lax.div(peer, rows), "rows": lax.rem(peer, rows)} for peer in peers]
+    barrier = pltpu.get_barrier_semaphore()
+    for place in places:
+        pl.semaphore_signal(barrier, inc=1, device_id=place, device_id_type=MESH)
+    pl.semaphore_wait(barrier, size - 1)
+    copies = []
+    for at, peer in enumerate(peers):
+        copy = pltpu.make_async_remote_copy(
+            src_ref=phi_ref.at[peer],
+            dst_ref=slots_ref.at[at],
+            send_sem=send_sem.at[at],
+            recv_sem=recv_sem.at[at],
+            device_id=places[at],
+            device_id_type=MESH,
+        )
+        copy.start()
+        copies.append(copy)
+    total = phi_ref[me]
+    for at, copy in enumerate(copies):
+        copy.wait()
+        total = total + slots_ref[at]
+    o_ref[...] = total
+
+
+def scatter_sum(phi, collective_id):
+    cols, rows = lax.axis_size("cols"), lax.axis_size("rows")
+    size = cols * rows
+    _, per, width = phi.shape
+    whole = pl.BlockSpec(memory_space=pltpu.VMEM)
+    return pl.pallas_call(
+        functools.partial(scatter_kernel, cols, rows),
+        in_specs=[whole],
+        out_specs=whole,
+        out_shape=jax.ShapeDtypeStruct((per, width), jnp.float32),
+        scratch_shapes=[
+            pltpu.VMEM((size - 1, per, width), jnp.float32),
+            pltpu.SemaphoreType.DMA((size - 1,)),
+            pltpu.SemaphoreType.DMA((size - 1,)),
+        ],
+        compiler_params=pltpu.CompilerParams(
+            collective_id=collective_id, has_side_effects=True, vmem_limit_bytes=32 * 2**20
+        ),
+    )(phi)
+
+
 def head_grads(embedded):
     clips = embedded.shape[2]
     exact = dict(precision=lax.Precision.HIGHEST, preferred_element_type=jnp.float32)
     raw = lax.dot_general(embedded[0], embedded[1], (((0,), (0,)), ((), ())), **exact)
     squares = jnp.sum(embedded * embedded, axis=1)
-    both = lax.psum(jnp.concatenate([raw, squares], axis=0), "cols")
-    inv_norm = 1.0 / jnp.sqrt(both[clips:] + 1e-06)
+    half = -(-(clips + 2) // 16) * 8
+    rest = jnp.zeros((2 * half - clips - 2, clips), jnp.float32)
+    packed = jnp.concatenate([raw, squares, rest], axis=0).reshape(2, half, clips)
+    both = sum_over(packed, "cols", 1).reshape(2 * half, clips)
+    inv_norm = 1.0 / jnp.sqrt(both[clips : clips + 2] + 1e-06)
     unit = embedded * inv_norm[:, None, :]
     cosine = both[:clips] * inv_norm[0][:, None] * inv_norm[1][None, :]
     expo = jnp.exp(logit_scale * cosine - logit_scale)
     row_soft = expo / jnp.sum(expo, axis=1, keepdims=True)
     col_soft = expo / jnp.sum(expo, axis=0, keepdims=True)
-    rest_row = 2.0 - jnp.diagonal(row_soft)
-    rest_col = 2.0 - jnp.diagonal(col_soft)
-    own = jnp.diagonal(cosine)
+    same = jnp.arange(clips)[:, None] == jnp.arange(clips)[None, :]
+    rest_row = 2.0 - jnp.sum(jnp.where(same, row_soft, 0.0), axis=0)
+    rest_col = 2.0 - jnp.sum(jnp.where(same, col_soft, 0.0), axis=0)
+    own = jnp.sum(jnp.where(same, cosine, 0.0), axis=0)
     half_scale = 0.5 * logit_scale
     pull_audio = lax.dot_general(unit[1], row_soft, (((1,), (1,)), ((), ())), **exact)
     pull_video = lax.dot_general(unit[0], col_soft, (((1,), (0,)), ((), ())), **exact)
@@ -134,11 +250,12 @@
     chosen = (owner_slot[None, :] == slots[:, None]).astype(jnp.bfloat16)
     x = jnp.einsum("mia,si->mas", clip_inputs, chosen, preferred_element_type=jnp.float32).astype(jnp.bfloat16)
     partial_value = jnp.einsum("mab,mas->mbs", head_weights, x, preferred_element_type=jnp.float32)
-    grads = head_grads(lax.psum(partial_value, "rows"))
+    grads = head_grads(sum_over(partial_value, "rows", 0))
     base = sign_seed * jnp.int32(GOLDEN) + (k_start * (2 * D * D) + a_start * D + b_start).astype(jnp.int32)
     phi = project(base, x, grads, k_part)
-    phi = jnp.transpose(phi.reshape(RESIDUES, -1, clip_count), (2, 1, 0)).reshape(clip_count, k_part)
-    return lax.psum_scatter(phi, ("cols", "rows"), scatter_dimension=0, tiled=True)
+    phi = jnp.transpose(phi.reshape(RESIDUES, -1, clip_count), (2, 1, 0))
+    owners = lax.axis_size("cols") * lax.axis_size("rows")
+    return scatter_sum(phi.reshape(owners, clip_count // owners, k_part), 2)
 
 
 def solution(mesh):

time: 304 us -> 195 us (0.64)
  waiting for transfers between devices: 129 us -> 0 us
  Pallas kernels: 143 us -> 185 us
  between operations: 13.9 us -> 0.85 us
  local copies, waits for them, and re-layouts: 9.38 us -> 2.44 us
    psum x2 -> x0, waiting for transfers between devices: 66.3 us -> none  [the longest x1 34.9 us: head_grads(): both = lax.psum(jnp.concatenate([raw, squares], axis=0), 'cols')]
    reduce_scatter x1 -> x0, waiting for transfers between devices: 62.5 us -> none  [per_device(): lax.psum_scatter(phi, ('cols', 'rows'), scatter_dimension=0, tiled=True)]
    pallas_call x0 -> x3, Pallas kernels: none -> 41.4 us  [the longest x2 26.4 us: sum_over(): pl.pallas_call(functools.partial(sum_kernel, axis, size), in_specs=[whole...]
    gather x3 -> x0, local copies, waits for them, and re-layouts: 7.03 us -> none  [the longest x1 2.34 us: head_grads(): own = jnp.diagonal(cosine)]
  transfers between devices with their start and end apart: 3 -> 0, of which waited for: 3 -> 0; matrix products, arithmetic and copies ran while one was open for 0% -> 0% of each run, Pallas kernels for 0% -> 0%
where the time goes in v2:
time: 195 us; the launch traced here: 193 us
  Pallas kernels  185 us (95%)
  matrix products  4.04 us (2%)
  local copies, waits for them, and re-layouts  2.44 us (1%)
    pallas_call x1, Pallas kernels, project(): pl.pallas_call(project_kernel, grid=(RESIDUES, 2), in_specs=[pl.BlockSpec...  144 us
    pallas_call x2, Pallas kernels, sum_over(): pl.pallas_call(functools.partial(sum_kernel, axis, size), in_specs=[whole...  26.4 us
    pallas_call x1, Pallas kernels, scatter_sum(): pl.pallas_call(functools.partial(scatter_kernel, cols, rows), in_specs=[w...  15.1 us

profile of v2, /device:TPU:0, one launch (start us, length us, event | category | flops | bytes accessed | tf_op | source)
XLA Modules:
  0.0 193.3 jit_solution(7943127699237907460)
XLA Ops:
  0.0 0.0 copy-start
  0.7 0.1 pad.6.clone
  0.8 0.3 copy-done
  1.1 1.0 fusion.x_ref
  2.1 1.4 convolution_bitcast_fusion.part_ref
  3.5 11.2 %shard_map.46 = f32[2,256,256]{2,1,0:T(8,128)S(1)} custom-call(f32[2,256,256]{2,1,0:T(8,128)S(1)} %convolution_bitcast_fusion.part_ref), custom_call_target="tpu_custom_call" | custom-call | tf_op jit(solution)/shard_map/pallas_call | solution.py:145
  14.7 0.1 multiply_reduce_fusion
  14.7 0.6 fusion.7
  15.3 0.1 maximum_maximum_fusion
  15.5 15.2 %shard_map.47 = f32[2,136,256]{2,1,0:T(8,128)S(1)} custom-call(f32[2,136,256]{2,1,0:T(8,128)S(1)} %bitcast.51), custom_call_target="tpu_custom_call" | custom-call | tf_op jit(solution)/shard_map/pallas_call | solution.py:145
  30.7 0.2 fusion.15
  30.9 0.3 multiply_reduce_fusion.2
  31.3 0.5 fusion.1
  31.8 0.5 fusion.2
  32.3 0.1 fusion.5.g_ref
  32.4 143.7 %shard_map.48 = f32[16,4,8,256]{3,2,1,0:T(8,128)S(1)} custom-call(s32[1]{0:T(128)S(6)} %add.22.base_ref, bf16[2,512,256]{2,1,0:T(8,128)(2,1)S(1)} %fusion.x_ref, bf16[2,256,256]{2,1,0:T(8,128)(2,1)S(1)} %fusion.5.g_ref), custom_call_target="tpu_custom_call" | custom-call | tf_op jit(solution)/shard_map/pallas_call | solution.py:87
  176.1 0.3 copy.18
  176.4 0.5 reshape.98
  176.9 0.7 copy.13.phi_ref
  177.6 15.1 %shard_map.49 = f32[32,512]{1,0:T(8,128)S(1)} custom-call(f32[8,32,512]{2,1,0:T(8,128)S(1)} %copy.13.phi_ref), custom_call_target="tpu_custom_call" | custom-call | tf_op jit(solution)/shard_map/pallas_call | solution.py:196
  192.7 0.6 copy.21
  (6 shorter events, 0.1 us)
Async XLA Ops:
  0.0 1.1 copy-start

commit v3 on v2

--- a/solution.py
+++ b/solution.py
@@ -12,7 +12,7 @@
 MIXER = 73244475
 GOLDEN = -1640531535
 RESIDUES = 16
-GROUP = 8
+GROUP = 16
 
 logit_scale = 14.0
 
@@ -26,7 +26,7 @@
     return lax.shift_right_logical(value, jnp.full((), amount, value.dtype))
 
 
-def project_kernel(base_ref, x_ref, g_ref, o_ref, top_ref, low_ref, add_ref, gain_ref, even_ref, odd_ref):
+def project_kernel(base_ref, x_ref, g_ref, o_ref, top_ref, low_ref, add_ref, gain_ref, sign_ref):
     res = pl.program_id(0)
     m = pl.program_id(1)
     b_part, a_part = top_ref.shape
@@ -67,16 +67,12 @@
         total = jnp.sum(jnp.sum(terms, axis=1), axis=1)
         o_ref[res, step] = jnp.where(m == 0, 0.0, o_ref[res, step]) + total
 
-    fill(even_ref, 0)
-
-    def body(t, carry):
-        use(even_ref, 2 * t)
-        fill(odd_ref, 2 * t + 1)
-        use(odd_ref, 2 * t + 1)
-        fill(even_ref, 2 * t + 2)
+    def body(step, carry):
+        fill(sign_ref, step)
+        use(sign_ref, step)
         return carry
 
-    lax.fori_loop(0, steps // 2, body, 0)
+    lax.fori_loop(0, steps, body, 0)
 
 
 def project(base, x, g, k_count):
@@ -92,7 +88,7 @@
         out_shape=jax.ShapeDtypeStruct((RESIDUES, steps, GROUP, n), jnp.float32),
         scratch_shapes=[pltpu.VMEM((b_part, a_part), jnp.int16)] * 3
         + [pltpu.VMEM((b_part, n), jnp.float32)]
-        + [pltpu.VMEM((GROUP * b_part, a_part), jnp.bfloat16)] * 2,
+        + [pltpu.VMEM((GROUP * b_part, a_part), jnp.bfloat16)],
         compiler_params=pltpu.CompilerParams(vmem_limit_bytes=48 * 2**20),
     )(base, x, g)
 

time: 195 us -> 182 us (0.933)
  Pallas kernels: 185 us -> 172 us
    pallas_call x1, Pallas kernels: 144 us -> 130 us  [project(): pl.pallas_call(project_kernel, grid=(RESIDUES, 2), in_specs=[pl.BlockSpec...]
where the time goes in v3:
time: 182 us; the launch traced here: 180 us
  Pallas kernels  172 us (95%)
  matrix products  4.04 us (2%)
  local copies, waits for them, and re-layouts  2.44 us (1%)
    pallas_call x1, Pallas kernels, project(): pl.pallas_call(project_kernel, grid=(RESIDUES, 2), in_specs=[pl.BlockSpec...  130 us
    pallas_call x2, Pallas kernels, sum_over(): pl.pallas_call(functools.partial(sum_kernel, axis, size), in_specs=[whole...  26.4 us
    pallas_call x1, Pallas kernels, scatter_sum(): pl.pallas_call(functools.partial(scatter_kernel, cols, rows), in_specs=[w...  15.1 us

profile of v3, /device:TPU:0, one launch (start us, length us, event | category | flops | bytes accessed | tf_op | source)
XLA Modules:
  0.0 179.9 jit_solution(16550145636242881488)
XLA Ops:
  0.0 0.0 copy-start
  0.7 0.1 pad.6.clone
  0.8 0.3 copy-done
  1.1 1.0 fusion.x_ref
  2.1 1.4 convolution_bitcast_fusion.part_ref
  3.5 11.2 %shard_map.46 = f32[2,256,256]{2,1,0:T(8,128)S(1)} custom-call(f32[2,256,256]{2,1,0:T(8,128)S(1)} %convolution_bitcast_fusion.part_ref), custom_call_target="tpu_custom_call" | custom-call | tf_op jit(solution)/shard_map/pallas_call | solution.py:141
  14.7 0.1 multiply_reduce_fusion
  14.7 0.6 fusion.7
  15.3 0.1 maximum_maximum_fusion
  15.5 15.2 %shard_map.47 = f32[2,136,256]{2,1,0:T(8,128)S(1)} custom-call(f32[2,136,256]{2,1,0:T(8,128)S(1)} %bitcast.51), custom_call_target="tpu_custom_call" | custom-call | tf_op jit(solution)/shard_map/pallas_call | solution.py:141
  30.7 0.2 fusion.15
  30.9 0.3 multiply_reduce_fusion.2
  31.3 0.5 fusion.1
  31.8 0.5 fusion.2
  32.3 0.1 fusion.5.g_ref
  32.4 130.3 %shard_map.48 = f32[16,2,16,256]{3,2,1,0:T(8,128)S(1)} custom-call(s32[1]{0:T(128)S(6)} %add.22.base_ref, bf16[2,512,256]{2,1,0:T(8,128)(2,1)S(1)} %fusion.x_ref, bf16[2,256,256]{2,1,0:T(8,128)(2,1)S(1)} %fusion.5.g_ref), custom_call_target="tpu_custom_call" | custom-call | tf_op jit(solution)/shard_map/pallas_call | solution.py:83
  162.7 0.3 copy.18
  163.0 0.5 reshape.98
  163.5 0.7 copy.13.phi_ref
  164.2 15.1 %shard_map.49 = f32[32,512]{1,0:T(8,128)S(1)} custom-call(f32[8,32,512]{2,1,0:T(8,128)S(1)} %copy.13.phi_ref), custom_call_target="tpu_custom_call" | custom-call | tf_op jit(solution)/shard_map/pallas_call | solution.py:192
  179.3 0.6 copy.21
  (6 shorter events, 0.1 us)
Async XLA Ops:
  0.0 1.1 copy-start
